TPU v7x, 32 devices: a whole 2x2x4 slice. The times are simulated.
32 devices in a mesh: rep: 8 (over z, y), slab: 4 (over x, core).
Axes of the slice: x: 2, y: 2, z: 4, core: 2. Of those that a mesh axis runs over, the one named last changes fastest.
Arguments:
- replica_field: float32 [16, 64, 128, 128], P('rep', 'slab')
- momentum: float32 [16, 64, 128, 128], P('rep', 'slab'), may hold values from -5 to 5
- parent: int32 [16], replicated, may hold values from 0 to 15, as said below
Outputs:
- field_out: float32 [16, 64, 128, 128], P('rep', 'slab')
- momentum_out: float32 [16, 64, 128, 128], P('rep', 'slab')
- action_density: float32 [16], P('rep')
Inputs may be any that keep to these rules, and one draw needn't show every extreme that they name: `parent`: exactly 4 entries differ from their own index, at most one among each aligned block of 2 entries; every entry that differs names an index whose own entry equals it.
All inputs are finite; a program needn't handle non-finite values.
Results may differ from a plain program's by a relative error of at most 0.00002.
Values sent between devices are 32-bit elements; how exact they have to be, the bound alone decides.
A program may use at most 128 MiB of HBM per device.

v0:
```python
import jax
import jax.numpy as jnp
from jax import lax
from jax.sharding import PartitionSpec as P

coupling = 0.5
mass_square = -1.0
step_size = 0.15


def padded(shard, sides, width):
    for axis, dim in sides:
        devices, length = (lax.axis_size(axis), shard.shape[dim])
        up = [(i, (i + 1) % devices) for i in range(devices)]
        down = [(j, i) for i, j in up]
        last = lax.slice_in_dim(shard, length - width, length, axis=dim)
        initial = lax.slice_in_dim(shard, 0, width, axis=dim)
        before = lax.ppermute(last, axis, up)
        after = lax.ppermute(initial, axis, down)
        shard = jnp.concatenate([before, shard, after], axis=dim)
    return shard


def force_inner(extended):
    center = extended[:, 1:-1]
    nearby = extended[:, :-2] + extended[:, 2:]
    nearby = nearby + jnp.roll(center, 1, 2) + jnp.roll(center, -1, 2)
    nearby = nearby + jnp.roll(center, 1, 3) + jnp.roll(center, -1, 3)
    return nearby - 6.0 * center - mass_square * center - coupling * center * center * center


def action_inner(extended):
    center = extended[:, 1:-1]
    along_z = extended[:, 2:] - center
    along_x = jnp.roll(center, -1, 2) - center
    along_y = jnp.roll(center, -1, 3) - center
    local = 0.5 * (along_z * along_z + along_x * along_x + along_y * along_y)
    local = (
        local
        + 0.5 * mass_square * center * center
        + 0.25 * coupling * center * center * center * center
    )
    return jnp.sum(local, axis=(1, 2, 3))


def extend_one(values):
    return padded(values, (("slab", 1),), 1)


def shards(replica_field, momentum, parent):
    per_group = replica_field.shape[0]
    depth = replica_field.shape[1]
    width_x = replica_field.shape[2]
    width_y = replica_field.shape[3]
    flat = replica_field.reshape(per_group, depth, width_x * width_y)
    spread = lax.all_to_all(flat, "rep", split_axis=2, concat_axis=0, tiled=True)
    copied = jnp.take(spread, parent, axis=0)
    returned = lax.all_to_all(copied, "rep", split_axis=0, concat_axis=2, tiled=True)
    field_start = returned.reshape(per_group, depth, width_x, width_y)
    volume = depth * lax.axis_size("slab") * width_x * width_y
    extended = extend_one(field_start)
    partial_action = action_inner(extended)
    half_kick = momentum + 0.5 * step_size * force_inner(extended)
    field_mid = field_start + step_size * half_kick
    kicked = half_kick + step_size * force_inner(extend_one(field_mid))
    field_end = field_mid + step_size * kicked
    momentum_end = kicked + 0.5 * step_size * force_inner(extend_one(field_end))
    density = lax.psum(partial_action, "slab") / volume
    return (field_end, momentum_end, density)


def solution(mesh):
    in_specs = (P("rep", "slab", None, None), P("rep", "slab", None, None), P())
    out_specs = (P("rep", "slab", None, None), P("rep", "slab", None, None), P("rep"))
    return jax.shard_map(shards, mesh=mesh, in_specs=in_specs, out_specs=out_specs, check_vma=False)
```

profile of v0, /device:TPU:0, one launch (start us, length us, event | category | flops | bytes accessed | tf_op | source)
XLA Modules:
  0.0 263.2 jit_solution(2905499698528240161)
XLA Ops:
  0.6 13.8 %copy.8 = f32[2,16,128,128]{1,0,3,2:T(2,128)} copy(f32[2,16,128,128]{3,2,1,0:T(8,128)} %param.3) | data formatting | bytes 4194304 | tf_op args[0]
  14.5 24.7 %reshape.29 = f32[8,1,65536]{2,1,0:T(1,128)} reshape(f32[16384,2,16]{2,1,0:T(2,128)} %bitcast.14) | data formatting | bytes 4194304
  39.2 7.4 %all-to-all-start = ((f32[8,1,65536]{2,1,0:T(1,128)}), f32[8,1,65536]{2,1,0:T(1,128)S(1)}, u32[]{:S(2)}, u32[]{:S(2)}) async-start(f32[8,1,65536]{2,1,0:T(1,128)} %reshape.29), calls=%async_computation | async-start | bytes 4194304 | tf_op jit(solution)/shard_map/all_to_all | solution.py:56
  46.6 0.0 copy-done.4
  46.7 48.2 %all-to-all-done = f32[8,1,65536]{2,1,0:T(1,128)S(1)} async-done(((f32[8,1,65536]{2,1,0:T(1,128)}), f32[8,1,65536]{2,1,0:T(1,128)S(1)}, u32[]{:S(2)}, u32[]{:S(2)}) %all-to-all-start) | async-done | bytes 2097184 | tf_op jit(solution)/shard_map/all_to_all | solution.py:56
  94.9 0.0 copy-start.2
  94.9 1.3 copy-done.2
  96.2 0.5 broadcast.64
  96.7 7.2 %reduce = f32[8,65536]{1,0:T(8,128)S(1)} reduce(f32[8,1,65536]{2,1,0:T(1,128)} %copy-done.2, f32[]{:T(128)} %broadcast.64), dimensions={1}, to_apply=%all_to_all.24.reduce_sub_computation | reduce | bytes 4194308 | tf_op jit(solution)/shard_map/all_to_all | solution.py:56
  103.9 28.5 %reshape.30 = f32[16384,2,16]{2,1,0:T(2,128)} reshape(f32[8,65536]{1,0:T(8,128)S(1)} %reduce) | data formatting | bytes 4194304
  132.4 20.1 %copy.13 = f32[2,16,8,2048]{3,1,0,2:T(8,128)S(1)} copy(f32[2,16,8,2048]{1,0,3,2:T(2,128)} %bitcast.13) | data formatting | bytes 4194304 | tf_op jit(solution)/shard_map/all_to_all | solution.py:56
  152.5 2.0 gather_fusion
  154.5 1.9 broadcast_select_fusion
  156.4 51.8 %all_to_all.33 = f32[16,16,2048]{2,1,0:T(8,128)S(1)} all-to-all(f32[16,16,2048]{2,1,0:T(8,128)S(1)} %broadcast_select_fusion), channel_id=1, replica_groups=mesh['rep'=8,'slab'=4] {'rep'}, dimensions={0} | all-to-all | bytes 4194304 | tf_op jit(solution)/shard_map/all_to_all | solution.py:58
  208.2 2.5 copy.11
  210.7 1.7 reshape.19
  212.5 0.7 fusion.53
  213.2 0.5 fusion.52
  213.7 0.0 copy-start.3
  213.8 0.7 fusion.54
  214.5 0.3 collective-permute-start
  214.8 1.7 collective-permute-start.1
  216.6 2.6 collective-permute-done
  219.2 0.4 collective-permute-done.1
  219.6 0.0 copy-done.3
  219.6 3.4 %multiply_add_fusion.1 = (f32[2,16,128,128]{3,2,1,0:T(8,128)S(1)}, f32[2,16,128,128]{3,2,1,0:T(8,128)}) fusion(f32[2,16,128,128]{3,2,1,0:T(8,128)S(1)} %reshape.19, f32[2,16,128,128]{3,2,1,0:T(8,128)S(1)} %copy-done.3, f32[2,16,128,1]{3,2,1,0:T(8,128)S(1)} %get-tuple-element.34, f32[2,16,128,127]{3,2,1,0:T(8,128)S(1)} %get-tuple-element.36, ...), kind=kLoop, calls=%fused_computation.53 | loop fusion | flops 12058624 | bytes 17039360 | tf_op jit(solution)/shard_map/add | solution.py:64
  223.0 2.7 %fusion.47 = (f32[2,16,127,128]{3,2,1,0:T(8,128)}, f32[2,16,127,128]{3,2,1,0:T(8,128)}) fusion(f32[2,16,128,128]{3,2,1,0:T(8,128)S(1)} %get-tuple-element.5), kind=kLoop, calls=%fused_computation.66 | loop fusion | bytes 8323072 | tf_op jit(solution)/shard_map/jit(_roll_static)/slice | solution.py:27
  225.7 2.7 %fusion.49 = (f32[2,16,128,127]{3,2,1,0:T(8,128)}, f32[2,16,128,127]{3,2,1,0:T(8,128)}) fusion(f32[2,16,128,128]{3,2,1,0:T(8,128)S(1)} %get-tuple-element.5), kind=kLoop, calls=%fused_computation.68 | loop fusion | bytes 8323072 | tf_op jit(solution)/shard_map/jit(_roll_static)/slice | solution.py:28
  228.4 2.7 %fusion.48 = (f32[2,16,128,1]{3,2,1,0:T(8,128)}, f32[2,16,128,1]{3,2,1,0:T(8,128)}) fusion(f32[2,16,128,128]{3,2,1,0:T(8,128)S(1)} %get-tuple-element.5), kind=kLoop, calls=%fused_computation.67 | loop fusion | bytes 65536 | tf_op jit(solution)/shard_map/jit(_roll_static)/slice | solution.py:28
  231.1 1.8 fusion.11
  232.9 0.0 copy-done.1
  233.0 7.6 %psum.7 = f32[2]{0:T(128)S(1)} all-reduce(f32[2]{0:T(128)S(1)} %fusion.11), channel_id=1, replica_groups=mesh['rep'=8,'slab'=4] {'slab'}, use_global_device_ids=true, to_apply=%region_1.2 | all-reduce | flops 2 | bytes 16 | tf_op jit(solution)/shard_map/psum | solution.py:68
  240.5 0.0 collective-permute-start.2
  240.6 1.7 collective-permute-start.3
  242.3 0.5 broadcast_multiply_fusion
  242.8 2.3 collective-permute-done.2
  245.1 0.0 collective-permute-done.3
  245.1 8.1 %multiply_add_fusion = (f32[2,16,128,128]{3,2,1,0:T(8,128)S(1)}, f32[2,16,128,128]{3,2,1,0:T(8,128)S(1)}) fusion(f32[2,16,128,128]{3,2,1,0:T(8,128)} %copy-done.1, f32[2,16,128,128]{3,2,1,0:T(8,128)} %get-tuple-element.6, f32[2,16,128,1]{3,2,1,0:T(8,128)} %get-tuple-element.24, f32[2,16,128,127]{3,2,1,0:T(8,128)} %get-tuple-element.26, ...), kind=kLoop, calls=%fused_computation.52 | loop fusion | flops 12058624 | bytes 17039360 | tf_op jit(solution)/shard_map/add | solution.py:66
  253.3 0.0 copy-start
  253.3 0.6 fusion.42
  253.9 0.7 fusion.41
  254.6 0.8 fusion.40
  255.4 1.1 collective-permute-start.4
  256.5 0.7 collective-permute-start.5
  257.2 2.7 %collective-permute-done.4 = f32[2,1,128,128]{3,2,1,0:T(8,128)S(1)} collective-permute-done((f32[2,1,128,128]{3,2,1,0:T(8,128)S(1)}, f32[2,1,128,128]{3,2,1,0:T(8,128)S(1)}, u32[]{:S(2)}, u32[]{:S(2)}) %collective-permute-start.4) | collective-permute-done | bytes 131104 | tf_op jit(solution)/shard_map/ppermute | solution.py:18
  259.9 0.0 collective-permute-done.5
  259.9 0.0 copy-done
  259.9 3.3 %fusion.8 = f32[2,16,128,128]{3,2,1,0:T(8,128)} fusion(f32[2,16,128,128]{3,2,1,0:T(8,128)S(1)} %get-tuple-element.4, f32[2,16,128,128]{3,2,1,0:T(8,128)S(1)} %get-tuple-element.3, f32[2,1,128,128]{3,2,1,0:T(8,128)S(1)} %collective-permute-done.5, f32[2,1,128,128]{3,2,1,0:T(8,128)S(1)} %collective-permute-done.4, ...), kind=kLoop, calls=%fused_computation.14 | loop fusion | flops 11010048 | bytes 14942208 | tf_op jit(solution)/shard_map/add | solution.py:67
  (11 shorter events, 0.2 us)
Async XLA Ops:
  39.2 7.4 %copy-start.4 = (s32[16]{0:T(128)S(1)}, s32[16]{0:T(128)}, u32[]{:S(2)}) copy-start(s32[16]{0:T(128)} %param.5) | copy-start | bytes 196
  39.2 55.7 %all-to-all-start = ((f32[8,1,65536]{2,1,0:T(1,128)}), f32[8,1,65536]{2,1,0:T(1,128)S(1)}, u32[]{:S(2)}, u32[]{:S(2)}) async-start(f32[8,1,65536]{2,1,0:T(1,128)} %reshape.29), calls=%async_computation | async-start | bytes 4194304 | tf_op jit(solution)/shard_map/all_to_all | solution.py:56
  94.9 1.3 copy-start.2
  213.7 5.9 %copy-start.3 = (f32[2,16,128,128]{3,2,1,0:T(8,128)S(1)}, f32[2,16,128,128]{3,2,1,0:T(8,128)}, u32[]{:S(2)}) copy-start(f32[2,16,128,128]{3,2,1,0:T(8,128)} %param.4) | copy-start | bytes 6291460
  214.5 4.7 %collective-permute-start = (f32[2,1,128,128]{3,2,1,0:T(8,128)S(1)}, f32[2,1,128,128]{3,2,1,0:T(8,128)S(1)}, u32[]{:S(2)}, u32[]{:S(2)}) collective-permute-start(f32[2,1,128,128]{3,2,1,0:T(8,128)S(1)} %get-tuple-element.27), channel_id=1, source_target_pairs={{0,1},{1,2},{2,3},{3,0},{4,5},{5,6},{6,7},{7,4},{8,9},{9,10},{10,1... | collective-permute-start | bytes 393224 | tf_op jit(solution)/shard_map/ppermute | solution.py:18
  214.8 4.8 %collective-permute-start.1 = (f32[2,1,128,128]{3,2,1,0:T(8,128)S(1)}, f32[2,1,128,128]{3,2,1,0:T(8,128)S(1)}, u32[]{:S(2)}, u32[]{:S(2)}) collective-permute-start(f32[2,1,128,128]{3,2,1,0:T(8,128)S(1)} %get-tuple-element.28), channel_id=1, source_target_pairs={{1,0},{2,1},{3,2},{0,3},{5,4},{6,5},{7,6},{4,7},{9,8},{10,9},{11,1... | collective-permute-start | bytes 393224 | tf_op jit(solution)/shard_map/ppermute | solution.py:19
  223.0 9.9 %copy-start.1 = (f32[2,16,128,128]{3,2,1,0:T(8,128)}, f32[2,16,128,128]{3,2,1,0:T(8,128)S(1)}, u32[]{:S(2)}) copy-start(f32[2,16,128,128]{3,2,1,0:T(8,128)S(1)} %get-tuple-element.5) | copy-start | bytes 6291460
  240.5 4.6 %collective-permute-start.2 = (f32[2,1,128,128]{3,2,1,0:T(8,128)S(1)}, f32[2,1,128,128]{3,2,1,0:T(8,128)S(1)}, u32[]{:S(2)}, u32[]{:S(2)}) collective-permute-start(f32[2,1,128,128]{3,2,1,0:T(8,128)S(1)} %get-tuple-element.17), channel_id=1, source_target_pairs={{0,1},{1,2},{2,3},{3,0},{4,5},{5,6},{6,7},{7,4},{8,9},{9,10},{10,1... | collective-permute-start | bytes 393224 | tf_op jit(solution)/shard_map/ppermute | solution.py:18
  240.6 4.5 %collective-permute-start.3 = (f32[2,1,128,128]{3,2,1,0:T(8,128)S(1)}, f32[2,1,128,128]{3,2,1,0:T(8,128)S(1)}, u32[]{:S(2)}, u32[]{:S(2)}) collective-permute-start(f32[2,1,128,128]{3,2,1,0:T(8,128)S(1)} %get-tuple-element.18), channel_id=1, source_target_pairs={{1,0},{2,1},{3,2},{0,3},{5,4},{6,5},{7,6},{4,7},{9,8},{10,9},{11,1... | collective-permute-start | bytes 393224 | tf_op jit(solution)/shard_map/ppermute | solution.py:19
  253.3 6.6 %copy-start = (f32[2,16,128,128]{3,2,1,0:T(8,128)}, f32[2,16,128,128]{3,2,1,0:T(8,128)S(1)}, u32[]{:S(2)}) copy-start(f32[2,16,128,128]{3,2,1,0:T(8,128)S(1)} %get-tuple-element.3) | copy-start | bytes 6291460
  255.4 4.5 %collective-permute-start.4 = (f32[2,1,128,128]{3,2,1,0:T(8,128)S(1)}, f32[2,1,128,128]{3,2,1,0:T(8,128)S(1)}, u32[]{:S(2)}, u32[]{:S(2)}) collective-permute-start(f32[2,1,128,128]{3,2,1,0:T(8,128)S(1)} %get-tuple-element.15), channel_id=1, source_target_pairs={{0,1},{1,2},{2,3},{3,0},{4,5},{5,6},{6,7},{7,4},{8,9},{9,10},{10,1... | collective-permute-start | bytes 393224 | tf_op jit(solution)/shard_map/ppermute | solution.py:18
  256.5 3.4 %collective-permute-start.5 = (f32[2,1,128,128]{3,2,1,0:T(8,128)S(1)}, f32[2,1,128,128]{3,2,1,0:T(8,128)S(1)}, u32[]{:S(2)}, u32[]{:S(2)}) collective-permute-start(f32[2,1,128,128]{3,2,1,0:T(8,128)S(1)} %get-tuple-element.16), channel_id=1, source_target_pairs={{1,0},{2,1},{3,2},{0,3},{5,4},{6,5},{7,6},{4,7},{9,8},{10,9},{11,1... | collective-permute-start | bytes 393224 | tf_op jit(solution)/shard_map/ppermute | solution.py:19
where the time goes:
time: 265 us; the launch traced here: 263 us
  local copies, waits for them, and re-layouts  108 us (41%)
  blocking collectives  59.4 us (22%)
  waiting for transfers between devices  56.2 us (21%)
  other arithmetic  26.2 us (10%)
  starting transfers between devices  13 us (5%)
    unnamed x13, local copies, waits for them, and re-layouts  68.4 us
    all_to_all x1, blocking collectives, shards(): lax.all_to_all(copied, 'rep', split_axis=0, concat_axis=2, tiled=True)  51.8 us
    all_to_all x1, waiting for transfers between devices, shards(): lax.all_to_all(flat, 'rep', split_axis=2, concat_axis=0, tiled=True)  48.2 us
    all_to_all x2, local copies, waits for them, and re-layouts, shards(): lax.all_to_all(flat, 'rep', split_axis=2, concat_axis=0, tiled=True)  20.6 us
    slice x6, local copies, waits for them, and re-layouts, force_inner(): nearby = nearby + jnp.roll(center, 1, 3) + jnp.roll(center, -1, 3)  8.38 us
    add x1, other arithmetic, shards(): field_end = field_mid + step_size * kicked  8.13 us
    ppermute x3, waiting for transfers between devices, padded(): before = lax.ppermute(last, axis, up)  7.6 us
    psum x1, blocking collectives, shards(): density = lax.psum(partial_action, 'slab') / volume  7.56 us
  transfers between devices with their start and end apart: 7, of which 5 were waited for; matrix products, arithmetic and copies ran while one was open for 0% of the time, Pallas kernels for 0%

commit v1 on v0

--- a/solution.py
+++ b/solution.py
@@ -1,11 +1,424 @@
+import functools
+
 import jax
 import jax.numpy as jnp
 from jax import lax
+from jax.experimental import pallas as pl
+from jax.experimental.pallas import tpu as pltpu
 from jax.sharding import PartitionSpec as P
 
 coupling = 0.5
 mass_square = -1.0
 step_size = 0.15
+
+ROWS = 4
+SPLIT = 2
+
+
+def holder_row(replica):
+    return replica // 4
+
+
+def links_needed(parent):
+    pair = parent.reshape(2 * ROWS, 2)
+    own = jnp.arange(4 * ROWS, dtype=jnp.int32).reshape(2 * ROWS, 2)
+    wanted = jnp.max(jnp.where(pair != own, pair, -1), axis=1).reshape(ROWS, 2)
+    names = jnp.arange(4 * ROWS, dtype=jnp.int32)
+    side = (names // 2) % 2
+    column = jnp.arange(2, dtype=jnp.int32)
+    across = jnp.any(wanted[None] == names[:, None, None], axis=1) & (side[:, None] != column[None])
+    most = jnp.max(jnp.sum(across.reshape(ROWS, 2, 2, 2).astype(jnp.int32), axis=2))
+    place = jnp.arange(ROWS, dtype=jnp.int32)
+    same = wanted[:, None] == wanted[None]
+    above = jnp.any(same & (place[None, :, None] > place[:, None, None]), axis=1)
+    below = jnp.any(same & (place[None, :, None] < place[:, None, None]), axis=1)
+    row = holder_row(wanted)
+    at = place[:, None, None]
+    dest = place[None, :, None]
+    valid = (wanted >= 0)[None]
+    up = valid & (dest > at) & (row[None] <= at) & ~above[None]
+    down = valid & (dest < at) & (row[None] >= at) & ~below[None]
+    most = jnp.maximum(most, jnp.max(jnp.sum(up.astype(jnp.int32), axis=1)))
+    return jnp.maximum(most, jnp.max(jnp.sum(down.astype(jnp.int32), axis=1)))
+
+
+def as_int(flag):
+    return jnp.where(flag, 1, 0).astype(jnp.int32)
+
+
+def line_items(wanted, at, passes, upward):
+    items = [jnp.int32(-1)] * passes
+    order = range(ROWS - 1, -1, -1) if upward else range(ROWS)
+    seen, count = [], jnp.int32(0)
+    for dest in order:
+        name = wanted[dest]
+        row = holder_row(name)
+        active = as_int(name >= 0)
+        if upward:
+            active = active * as_int(dest > at) * as_int(row <= at)
+        else:
+            active = active * as_int(dest < at) * as_int(row >= at)
+        for other in seen:
+            active = active * as_int(other != name)
+        for p in range(passes):
+            items[p] = jnp.where(active * as_int(count == p) == 1, name, items[p])
+        count = count + active
+        seen.append(name)
+    return items
+
+
+def cross_items(wanted, first, passes):
+    need = []
+    for local in range(2):
+        flag = jnp.int32(0)
+        for dest in range(ROWS):
+            flag = jnp.maximum(flag, as_int(wanted[dest] == first + local))
+        need.append(flag)
+    items = [jnp.where(need[0] == 1, first, jnp.where(need[1] == 1, first + 1, -1))]
+    if passes > 1:
+        items.append(jnp.where(need[0] * need[1] == 1, first + 1, -1))
+    return items
+
+
+def pick(name, candidates):
+    value = candidates[0][1]
+    for other, block in candidates[1:]:
+        value = jnp.where(other == name, block, value)
+    return value
+
+
+def force(lower, center, upper):
+    top = pltpu.roll(center, center.shape[0] - 1, 0)
+    bottom = pltpu.roll(center, 1, 0)
+    right = pltpu.roll(center, center.shape[1] - 1, 1)
+    left = pltpu.roll(center, 1, 1)
+    nearby = (lower + upper) + (top + bottom) + (right + left)
+    value = nearby - center * ((6.0 + mass_square) + coupling * (center * center))
+    return value, top, right
+
+
+def kernel(passes, slabs, delay, volume,
+           parent_ref, field_ref, mom_ref, out_f, out_m, out_a,
+           own, moved, mom, kick, mid, kick_b, end, rest_f, rest_m, sums, tiles, tiles_in,
+           y_out, y_in, up_out, up_in, dn_out, dn_in,
+           load_sem, halo_s, halo_r, y_s, y_r, up_s, up_r, dn_s, dn_r, act_s, act_r):
+    depth, wx, wy = field_ref.shape[1:]
+    chunks = depth * SPLIT
+    part = wx // SPLIT
+    cross = min(passes, 2)
+    rep = lax.axis_index("rep")
+    slab = lax.axis_index("slab")
+    z = rep // 2
+    y = rep % 2
+    partner = rep + 1 - 2 * y
+    above = lax.rem(slab + 1, slabs)
+    below = lax.rem(slab + slabs - 1, slabs)
+
+    loads = [
+        pltpu.make_async_copy(field_ref, own.at[:, 3:3 + depth], load_sem.at[0]),
+        pltpu.make_async_copy(mom_ref, mom.at[:, 2:2 + depth], load_sem.at[1]),
+    ]
+    for copy in loads:
+        copy.start()
+
+    barrier = pltpu.get_barrier_semaphore()
+
+    def greet(device):
+        pl.semaphore_signal(barrier, inc=1, device_id=device, device_id_type=pl.DeviceIdType.MESH)
+
+    for far in range(1, slabs):
+        greet((rep, lax.rem(slab + far, slabs)))
+    greet((partner, slab))
+
+    @pl.when(z > 0)
+    def _():
+        greet((rep - 2, slab))
+
+    @pl.when(z < ROWS - 1)
+    def _():
+        greet((rep + 2, slab))
+
+    pl.semaphore_wait(barrier, slabs + as_int(z > 0) + as_int(z < ROWS - 1))
+
+    def remote(src, dst, send, recv, device):
+        return pltpu.make_async_remote_copy(
+            src_ref=src, dst_ref=dst, send_sem=send, recv_sem=recv,
+            device_id=device, device_id_type=pl.DeviceIdType.MESH)
+
+    halos = [
+        remote(field_ref.at[:, depth - 3:depth], own.at[:, 0:3], halo_s.at[0], halo_r.at[0], (rep, above)),
+        remote(field_ref.at[:, 0:3], own.at[:, depth + 3:depth + 6], halo_s.at[1], halo_r.at[1], (rep, below)),
+        remote(mom_ref.at[:, depth - 2:depth], mom.at[:, 0:2], halo_s.at[2], halo_r.at[2], (rep, above)),
+        remote(mom_ref.at[:, 0:2], mom.at[:, depth + 2:depth + 4], halo_s.at[3], halo_r.at[3], (rep, below)),
+    ]
+    for copy in halos:
+        copy.start()
+    moved_halos = [
+        remote(moved.at[depth:depth + 3], moved.at[0:3], halo_s.at[4], halo_r.at[4], (rep, above)),
+        remote(moved.at[3:6], moved.at[depth + 3:depth + 6], halo_s.at[5], halo_r.at[5], (rep, below)),
+    ]
+
+    by_group = []
+    slots = []
+    for group in range(2 * ROWS):
+        first, second = parent_ref[2 * group], parent_ref[2 * group + 1]
+        by_group.append(jnp.where(first != 2 * group, first, jnp.where(second != 2 * group + 1, second, -1)))
+        slots.append(as_int(second != 2 * group + 1))
+    mine, other = [], []
+    for row in range(ROWS):
+        mine.append(jnp.where(y == 0, by_group[2 * row], by_group[2 * row + 1]))
+        other.append(jnp.where(y == 0, by_group[2 * row + 1], by_group[2 * row]))
+    here, slot = jnp.int32(-1), jnp.int32(0)
+    for group in range(2 * ROWS):
+        here = jnp.where(rep == group, by_group[group], here)
+        slot = jnp.where(rep == group, slots[group], slot)
+    here = jnp.where(here >= 0, here, 2 * rep)
+    y_out_items = cross_items(other, 2 * rep, cross)
+    y_in_items = cross_items(mine, 2 * partner, cross)
+    up_out_items = line_items(mine, z, passes, True)
+    up_in_items = line_items(mine, z - 1, passes, True)
+    dn_out_items = line_items(mine, z, passes, False)
+    dn_in_items = line_items(mine, z + 1, passes, False)
+
+    def copy_y(c):
+        return remote(y_out.at[c], y_in.at[c], y_s.at[c], y_r.at[c], (partner, slab))
+
+    def copy_up(c):
+        return remote(up_out.at[c], up_in.at[c], up_s.at[c], up_r.at[c], (rep + 2, slab))
+
+    def copy_dn(c):
+        return remote(dn_out.at[c], dn_in.at[c], dn_s.at[c], dn_r.at[c], (rep - 2, slab))
+
+    def layer_of(c):
+        k = c // SPLIT
+        return jnp.where(k < 3, k, jnp.where(k < 6, k + depth - 6, k - 3))
+
+    def rows_of(c):
+        return pl.ds(pl.multiple_of((c % SPLIT) * part, part), part)
+
+    def own_blocks(c):
+        layer, rows = layer_of(c), rows_of(c)
+        return [(2 * rep, own[0, 3 + layer, rows]), (2 * rep + 1, own[1, 3 + layer, rows])]
+
+    def cross_blocks(c):
+        return [(y_in_items[q], y_in[c, q]) for q in range(cross)]
+
+    def up_blocks(c):
+        return [(up_in_items[q], up_in[c, q]) for q in range(passes)]
+
+    def dn_blocks(c):
+        return [(dn_in_items[q], dn_in[c, q]) for q in range(passes)]
+
+    def layer_step(k, field_at, mom_at, which, emit):
+        center = field_at(k)
+        upper = field_at(k + 1)
+        value, top, right = force(field_at(k - 1), center, upper)
+        first = mom_at(k - 1) + (0.5 * step_size) * value
+        kick[k] = first
+        mid[k] = center + step_size * first
+
+        @pl.when((k >= 3) & (k < depth + 3))
+        def _():
+            dz, dx, dy = upper - center, top - center, right - center
+            square = center * center
+            local = 0.5 * (dz * dz + dx * dx + dy * dy)
+            local = local + square * (0.5 * mass_square + (0.25 * coupling) * square)
+            sums[which] += jnp.sum(local.reshape(wx // 8, 8, wy), axis=0)
+
+        @pl.when(k >= 3)
+        def _():
+            at = mid[k - 1]
+            value, _, _ = force(mid[k - 2], at, mid[k])
+            second = kick[k - 1] + step_size * value
+            kick_b[k - 1] = second
+            end[k - 1] = at + step_size * second
+
+        @pl.when(k >= 5)
+        def _():
+            at = end[k - 2]
+            value, _, _ = force(end[k - 3], at, end[k - 1])
+            emit(k - 5, at, kick_b[k - 2] + (0.5 * step_size) * value)
+
+    sums[...] = jnp.zeros_like(sums)
+    loads[0].wait()
+    loads[1].wait()
+    rest = 1 - slot
+    steps = depth + 4
+    total = chunks + ROWS * delay
+    begin_rest = total - steps
+    up_skew = delay * (z + 1)
+    dn_skew = delay * (ROWS - z)
+    end_skew = jnp.maximum(up_skew, dn_skew)
+
+    def rest_emit(layer, field, momentum):
+        rest_f[layer] = field
+        rest_m[layer] = momentum
+
+    def during(t, skew):
+        return (t >= skew) & (t < skew + chunks)
+
+    def step(t, _):
+        @pl.when(t < chunks)
+        def _():
+            blocks = own_blocks(t)
+            for p in range(cross):
+                y_out[t, p] = pick(y_out_items[p], blocks)
+            copy_y(t).start()
+
+        @pl.when(during(t, delay))
+        def _():
+            copy_y(t - delay).wait_recv()
+
+        @pl.when(during(t, up_skew) & (z > 0))
+        def _():
+            copy_up(t - up_skew).wait_recv()
+
+        @pl.when(during(t, dn_skew) & (z < ROWS - 1))
+        def _():
+            copy_dn(t - dn_skew).wait_recv()
+
+        @pl.when(during(t, up_skew) & (z < ROWS - 1))
+        def _():
+            c = t - up_skew
+            blocks = own_blocks(c) + cross_blocks(c) + up_blocks(c)
+            for p in range(passes):
+                up_out[c, p] = pick(up_out_items[p], blocks)
+            copy_up(c).start()
+
+        @pl.when(during(t, dn_skew) & (z > 0))
+        def _():
+            c = t - dn_skew
+            blocks = own_blocks(c) + cross_blocks(c) + dn_blocks(c)
+            for p in range(passes):
+                dn_out[c, p] = pick(dn_out_items[p], blocks)
+            copy_dn(c).start()
+
+        @pl.when(during(t, end_skew))
+        def _():
+            c = t - end_skew
+            blocks = own_blocks(c) + cross_blocks(c) + up_blocks(c) + dn_blocks(c)
+            moved[3 + layer_of(c), rows_of(c)] = pick(here, blocks)
+
+        @pl.when(t == end_skew + 6 * SPLIT - 1)
+        def _():
+            for copy in moved_halos:
+                copy.start()
+
+        @pl.when(t == begin_rest)
+        def _():
+            for copy in halos:
+                copy.wait_recv()
+
+        @pl.when(t >= begin_rest)
+        def _():
+            layer_step(t - begin_rest + 1, lambda k: own[rest, k], lambda k: mom[rest, k], 0, rest_emit)
+
+        return 0
+
+    lax.fori_loop(0, total, step, 0)
+    for copy in moved_halos:
+        copy.wait_recv()
+
+    def moved_emit(layer, field, momentum):
+        other_f, other_m = rest_f[layer], rest_m[layer]
+        out_f[0, layer] = jnp.where(slot == 0, field, other_f)
+        out_f[1, layer] = jnp.where(slot == 0, other_f, field)
+        out_m[0, layer] = jnp.where(slot == 0, momentum, other_m)
+        out_m[1, layer] = jnp.where(slot == 0, other_m, momentum)
+
+    def moved_step(k, _):
+        layer_step(k, lambda i: moved[i], lambda i: mom[slot, i], 1, moved_emit)
+        return 0
+
+    lax.fori_loop(1, steps + 1, moved_step, 0)
+
+    tiles[0] = jnp.where(slot == 0, sums[1], sums[0])
+    tiles[1] = jnp.where(slot == 0, sums[0], sums[1])
+    shares = [
+        remote(tiles, tiles_in.at[far - 1], act_s.at[far - 1], act_r.at[far - 1],
+               (rep, lax.rem(slab + far, slabs)))
+        for far in range(1, slabs)
+    ]
+    for copy in shares:
+        copy.start()
+
+    for copy in halos + moved_halos:
+        copy.wait_send()
+
+    def drain(c, _):
+        copy_y(c).wait_send()
+
+        @pl.when(z < ROWS - 1)
+        def _():
+            copy_up(c).wait_send()
+
+        @pl.when(z > 0)
+        def _():
+            copy_dn(c).wait_send()
+
+        return 0
+
+    lax.fori_loop(0, chunks, drain, 0)
+    for copy in shares:
+        copy.wait()
+    whole = tiles[...]
+    for far in range(1, slabs):
+        whole = whole + tiles_in[far - 1]
+    out_a[0] = jnp.sum(whole[0]) * (1.0 / volume)
+    out_a[1] = jnp.sum(whole[1]) * (1.0 / volume)
+
+
+def run(passes, slabs, delay, replica_field, momentum, parent):
+    pair, depth, wx, wy = replica_field.shape
+    chunks = depth * SPLIT
+    part = wx // SPLIT
+    cross = min(passes, 2)
+    f32 = jnp.float32
+
+    def plane(*lead):
+        return pltpu.VMEM((*lead, wx, wy), f32)
+
+    def block(count):
+        return pltpu.VMEM((chunks, count, part, wy), f32)
+
+    dma = pltpu.SemaphoreType.DMA
+    volume = depth * slabs * wx * wy
+    return pl.pallas_call(
+        functools.partial(kernel, passes, slabs, delay, volume),
+        out_shape=(
+            jax.ShapeDtypeStruct(replica_field.shape, f32),
+            jax.ShapeDtypeStruct(replica_field.shape, f32),
+            jax.ShapeDtypeStruct((pair,), f32),
+        ),
+        in_specs=[
+            pl.BlockSpec(memory_space=pltpu.SMEM),
+            pl.BlockSpec(memory_space=pl.ANY),
+            pl.BlockSpec(memory_space=pl.ANY),
+        ],
+        out_specs=(
+            pl.BlockSpec(memory_space=pltpu.VMEM),
+            pl.BlockSpec(memory_space=pltpu.VMEM),
+            pl.BlockSpec(memory_space=pltpu.SMEM),
+        ),
+        scratch_shapes=[
+            plane(pair, depth + 6), plane(depth + 6), plane(pair, depth + 4),
+            plane(depth + 6), plane(depth + 6), plane(depth + 6), plane(depth + 6),
+            plane(depth), plane(depth),
+            pltpu.VMEM((2, 8, wy), f32), pltpu.VMEM((2, 8, wy), f32), pltpu.VMEM((slabs - 1, 2, 8, wy), f32),
+            block(cross), block(cross), block(passes), block(passes), block(passes), block(passes),
+            dma((2,)), dma((6,)), dma((6,)),
+            dma((chunks,)), dma((chunks,)), dma((chunks,)), dma((chunks,)), dma((chunks,)), dma((chunks,)),
+            dma((slabs - 1,)), dma((slabs - 1,)),
+        ],
+        compiler_params=pltpu.CompilerParams(
+            collective_id=passes, has_side_effects=True, vmem_limit_bytes=56 * 2**20),
+    )(parent, replica_field, momentum)
+
+
+def routed(replica_field, momentum, parent):
+    slabs = lax.axis_size("slab")
+    branches = [functools.partial(run, passes, slabs, delay) for passes, delay in ((1, 3), (2, 2), (3, 2))]
+    return lax.switch(links_needed(parent) - 1, branches, replica_field, momentum, parent)
 
 
 def padded(shard, sides, width):
@@ -72,4 +485,5 @@
 def solution(mesh):
     in_specs = (P("rep", "slab", None, None), P("rep", "slab", None, None), P())
     out_specs = (P("rep", "slab", None, None), P("rep", "slab", None, None), P("rep"))
-    return jax.shard_map(shards, mesh=mesh, in_specs=in_specs, out_specs=out_specs, check_vma=False)
+    plan = routed if mesh.shape["rep"] == 2 * ROWS and mesh.shape["slab"] > 2 else shards
+    return jax.shard_map(plan, mesh=mesh, in_specs=in_specs, out_specs=out_specs, check_vma=False)

time: 265 us -> 101 us (0.38)
  local copies, waits for them, and re-layouts: 108 us -> 5.37 us
  Pallas kernels: 0 us -> 90.3 us
  blocking collectives: 59.4 us -> 0 us
  waiting for transfers between devices: 56.2 us -> 0 us
  other arithmetic: 26.2 us -> 2.78 us
  starting transfers between devices: 13 us -> 0 us
    pallas_call x0 -> x1, Pallas kernels: none -> 90.3 us  [run(): pl.pallas_call(functools.partial(kernel, passes, slabs, delay, volume), o...]
    unnamed x13 -> x5, local copies, waits for them, and re-layouts: 68.4 us -> 4.17 us
    all_to_all x1 -> x0, blocking collectives: 51.8 us -> none  [shards(): lax.all_to_all(copied, 'rep', split_axis=0, concat_axis=2, tiled=True)]
    all_to_all x1 -> x0, waiting for transfers between devices: 48.2 us -> none  [shards(): lax.all_to_all(flat, 'rep', split_axis=2, concat_axis=0, tiled=True)]
    all_to_all x3 -> x0, local copies, waits for them, and re-layouts: 23.2 us -> none  [the longest x2 20.6 us: shards(): lax.all_to_all(flat, 'rep', split_axis=2, concat_axis=0, tiled=True)]
    add x3 -> x0, other arithmetic: 14.8 us -> none  [the longest x1 8.13 us: shards(): field_end = field_mid + step_size * kicked]
    slice x15 -> x0, local copies, waits for them, and re-layouts: 12.2 us -> none  [the longest x6 8.38 us: force_inner(): nearby = nearby + jnp.roll(center, 1, 3) + jnp.roll(center, -1, 3)]
    ppermute x6 -> x0, waiting for transfers between devices: 8.02 us -> none  [the longest x3 7.6 us: padded(): before = lax.ppermute(last, axis, up)]
  transfers between devices with their start and end apart: 7 -> 0, of which waited for: 5 -> 0; matrix products, arithmetic and copies ran while one was open for 0% -> 0% of each run, Pallas kernels for 0% -> 0%
where the time goes in v1:
time: 101 us
  Pallas kernels  90.3 us (89%)
  local copies, waits for them, and re-layouts  5.37 us (5%)
  other arithmetic  2.78 us (3%)
  between operations  2.63 us (3%)
    pallas_call x1, Pallas kernels, run(): pl.pallas_call(functools.partial(kernel, passes, slabs, delay, volume), o...  90.3 us
    unnamed x5, local copies, waits for them, and re-layouts  4.17 us

profile of v1, /device:TPU:0, one launch (start us, length us, event | category | flops | bytes accessed | tf_op | source)
XLA Modules:
  0.0 101.1 jit_solution(11308698855866438983)
XLA Ops:
  0.6 0.7 reshape.126
  1.4 0.1 fusion.2
  1.5 0.1 eq.30
  1.6 0.1 copy.22
  1.7 0.1 copy.21
  1.8 0.1 copy.23
  1.9 0.1 fusion.5
  2.0 0.2 fusion.4
  2.2 0.2 convert_reduce_fusion
  2.4 0.6 reduce_max.38
  3.0 0.6 reduce_max.39
  3.7 0.1 reduce_or.30
  3.8 0.2 fusion
  4.0 0.6 reduce_max.37
  6.6 90.3 %conditional.1 = ((f32[2,16,128,128]{3,2,1,0:T(8,128)S(1)}, f32[2,16,128,128]{3,2,1,0:T(8,128)}, f32[2]{0:T(128)S(1)})) conditional(s32[]{:T(128)} %clamp.3, (s32[16]{0:T(128)}, f32[2,16,128,128]{3,2,1,0:T(8,128)}, f32[2,16,128,128]{3,2,1,0:T(8,128)}) %tuple.16, (s32[16]{0:T(128)}, f32[2,16,128,128]{3,2,1,0:T(8,128)}, ...), branch_computations={%region_10.11_spmd, %region_11.12_spmd, %region_12.13_spmd} | conditional | bytes 8 | solution.py:421
  6.6 90.3 %branch_1_fun.1 = (f32[2,16,128,128]{3,2,1,0:T(8,128)S(1)}, f32[2,16,128,128]{3,2,1,0:T(8,128)}, f32[2]{0:T(128)S(1)}) custom-call(s32[16]{0:T(128)} %get-tuple-element.21.parent_ref, f32[2,16,128,128]{3,2,1,0:T(8,128)} %get-tuple-element.49.field_ref, f32[2,16,128,128]{3,2,1,0:T(8,128)} %get-tuple-element.52.mom_ref), custom_call_target="tpu_custom_call" | custom-call | tf_op jit(solution)/shard_map/cond/branch_1_fun/pallas_call | solution.py:386
  96.9 0.0 copy-start
  96.9 1.3 %copy.38 = f32[2,16,128,128]{3,2,1,0:T(8,128)} copy(f32[2,16,128,128]{3,2,1,0:T(8,128)S(1)} %get-tuple-element.72) | data formatting | bytes 4194304
  98.2 1.0 %copy-done = f32[2,16,128,128]{3,2,1,0:T(8,128)S(1)} copy-done((f32[2,16,128,128]{3,2,1,0:T(8,128)S(1)}, f32[2,16,128,128]{3,2,1,0:T(8,128)}, u32[]{:S(2)}) %copy-start) | copy-done | bytes 2097176
  99.3 1.3 %copy.39 = f32[2,16,128,128]{3,2,1,0:T(8,128)} copy(f32[2,16,128,128]{3,2,1,0:T(8,128)S(1)} %copy-done) | data formatting | bytes 4194304
  100.6 0.5 copy.40
  (6 shorter events, 0.1 us)
Async XLA Ops:
  96.9 2.3 %copy-start = (f32[2,16,128,128]{3,2,1,0:T(8,128)S(1)}, f32[2,16,128,128]{3,2,1,0:T(8,128)}, u32[]{:S(2)}) copy-start(f32[2,16,128,128]{3,2,1,0:T(8,128)} %get-tuple-element.73) | copy-start | bytes 6291460
